TPU v7x, 32 devices: a whole 2x2x4 slice. The times are simulated.
32 devices in a mesh: lon: 8 (over y, x, core), lat: 4 (over z).
Axes of the slice: x: 2, y: 2, z: 4, core: 2. Of those that a mesh axis runs over, the one named last changes fastest.
Arguments:
- direction: float32 [75, 32, 1024], P(None, 'lat', 'lon'), may hold values from -40 to 40
- residual: float32 [75, 32, 1024], P(None, 'lat', 'lon'), may hold values from -40 to 40
- eof_basis: float32 [75, 75], replicated, may hold values from -0.75 to 0.75
- kappa_east: float32 [32, 1024], P('lat', 'lon'), may hold values from 0.02 to 0.24
- kappa_north: float32 [32, 1024], P('lat', 'lon'), may hold values from 0.02 to 0.24
- wet_mask: int32 [32, 1024], P('lat', 'lon'), may hold values 0 or 1
- obs_base: int32 [4, 8, 256], P('lat', 'lon'), may hold values from 0 to 1023, as said below
- obs_frac: float32 [2, 4, 8, 256], P(None, 'lat', 'lon'), may hold values from 0 to 1
- obs_rinv: float32 [75, 4, 8, 256], P(None, 'lat', 'lon'), may hold values from 0.25 to 4
Outputs:
- new_residual: float32 [75, 32, 1024], P(None, 'lat', 'lon')
- new_direction: float32 [75, 32, 1024], P(None, 'lat', 'lon')
- step_length: float32 [], replicated
Inputs may be any that keep to these rules, and one draw needn't show every extreme that they name: `obs_base`: s // 128 and s % 128 are the row and column of the square's south-west cell within the tile; no profile of the top tile row has its south-west cell in the grid's top row.
All inputs are finite; a program needn't handle non-finite values. No bound on the sum of `wet_mask` on one device may be relied on, other than what follows from the above.
Results may differ from a plain program's by a relative error of at most 0.000066.
Values sent between devices are 32-bit elements; how exact they have to be, the bound alone decides.
A program may use at most 64 MiB of HBM per device.

v0:
```python
import jax
import jax.numpy as jnp
from jax import lax
from jax.sharding import PartitionSpec as P


def padded_2(array, sides, width):
    for axis, dim in sides:
        peers, length = (lax.axis_size(axis), array.shape[dim])
        up = [(i, (i + 1) % peers) for i in range(peers)]
        down = [(j, i) for i, j in up]
        last = lax.slice_in_dim(array, length - width, length, axis=dim)
        leading = lax.slice_in_dim(array, 0, width, axis=dim)
        before = lax.ppermute(last, axis, up)
        after = lax.ppermute(leading, axis, down)
        array = jnp.concatenate([before, array, after], axis=dim)
    return array


def swapped(array, axis, stride):
    return lax.ppermute(array, axis, [(i, i ^ 1 << stride) for i in range(lax.axis_size(axis))])


def passed_along(value, axis, steps):
    count = lax.axis_size(axis)
    pairs = [(source, (source + steps) % count) for source in range(count)]
    return lax.ppermute(value, axis, pairs)


def passed_along_2(value, axis, steps):
    count = lax.axis_size(axis)
    leading, last = (max(0, -steps), min(count, count - steps))
    return lax.ppermute(value, axis, [(source, source + steps) for source in range(leading, last)])


def with_rims(values):
    padded = padded_2(values, (("lon", 2), ("lat", 1)), 1)
    row_total = values.shape[1] + 2
    lat_index = lax.axis_index("lat")
    lat_count = lax.axis_size("lat")
    row_ids = jnp.arange(row_total)
    outside = (row_ids == 0) & (lat_index == 0) | (row_ids == row_total - 1) & (
        lat_index == lat_count - 1
    )
    return padded * jnp.where(outside, 0.0, 1.0).astype(jnp.float32)[None, :, None]


def mirror_row(top_rows):
    moved = top_rows
    for bit_index in range(lax.axis_size("lon").bit_length() - 1):
        moved = swapped(moved, "lon", bit_index)
    return moved[:, ::-1]


def diffuse(values, faces):
    east_face, west_face, north_face, south_face, fold_face = faces
    padded = with_rims(values)
    mirrored = mirror_row(values[:, -1, :])
    change = east_face * (padded[:, 1:-1, 2:] - values)
    change = change + west_face * (padded[:, 1:-1, :-2] - values)
    change = change + north_face * (padded[:, 2:, 1:-1] - values)
    change = change + south_face * (padded[:, :-2, 1:-1] - values)
    change = change.at[:, -1, :].add(fold_face * (mirrored - values[:, -1, :]))
    return values + change


def per_device(
    direction, residual, eof_basis, kappa_east, kappa_north, wet_mask, obs_base, obs_frac, obs_rinv
):
    levels, lat_cells, lon_cells = direction.shape
    old_norm = lax.psum(jnp.sum(residual * residual), ("lon", "lat"))
    wet_float = wet_mask.astype(jnp.float32)
    static = with_rims(jnp.stack([kappa_east, kappa_north, wet_float]))
    east_rim, north_rim, wet_rim = (static[0], static[1], static[2])
    east_full = east_rim[:, :-1] * wet_rim[:, :-1] * wet_rim[:, 1:]
    north_full = north_rim[:-1] * wet_rim[:-1] * wet_rim[1:]
    top_pair = mirror_row(jnp.stack([kappa_north[-1], wet_float[-1]]))
    is_top = jnp.where(lax.axis_index("lat") == lax.axis_size("lat") - 1, 1.0, 0.0).astype(
        jnp.float32
    )
    fold_face = is_top * 0.5 * (kappa_north[-1] + top_pair[0]) * wet_float[-1] * top_pair[1]
    faces = (
        east_full[1:-1, 1:],
        east_full[1:-1, :-1],
        north_full[1:, 1:-1],
        north_full[:-1, 1:-1],
        fold_face,
    )
    physical = jnp.dot(
        eof_basis,
        direction.reshape(levels, -1),
        precision=lax.Precision.HIGHEST,
        preferred_element_type=jnp.float32,
    ).reshape(direction.shape)
    for step_index in range(3):
        physical = diffuse(physical, faces)
    padded = with_rims(physical)
    row_width = lon_cells + 2
    flat_field = padded.reshape(levels, -1)
    base_flat = obs_base.reshape(-1)
    south_west = (base_flat // lon_cells + 1) * row_width + base_flat % lon_cells + 1
    corner_index = (south_west, south_west + 1, south_west + row_width, south_west + row_width + 1)
    frac_flat = obs_frac.reshape(2, -1)
    lat_frac = frac_flat[0]
    lon_frac = frac_flat[1]
    corner_weight = (
        (1.0 - lat_frac) * (1.0 - lon_frac),
        (1.0 - lat_frac) * lon_frac,
        lat_frac * (1.0 - lon_frac),
        lat_frac * lon_frac,
    )
    profiles = jnp.zeros((levels, base_flat.shape[0]), jnp.float32)
    for corner in range(4):
        profiles = profiles + corner_weight[corner][None, :] * jnp.take(
            flat_field, corner_index[corner], axis=1
        )
    weighted = obs_rinv.reshape(levels, -1) * profiles
    spread = jnp.zeros_like(flat_field)
    for corner in range(4):
        spread = spread.at[:, corner_index[corner]].add(corner_weight[corner][None, :] * weighted)
    spread = spread.reshape(padded.shape)
    east_part = spread[:, 1 : lat_cells + 2, lon_cells + 1]
    spread = spread.at[:, 1 : lat_cells + 2, 1].add(passed_along(east_part, "lon", 1))
    top_line = spread[:, lat_cells + 1, 1 : lon_cells + 1]
    adjoint = spread[:, 1 : lat_cells + 1, 1 : lon_cells + 1]
    adjoint = adjoint.at[:, 0, :].add(passed_along_2(top_line, "lat", 1))
    for step_index in range(3):
        adjoint = diffuse(adjoint, faces)
    back_term = jnp.dot(
        eof_basis.T,
        adjoint.reshape(levels, -1),
        precision=lax.Precision.HIGHEST,
        preferred_element_type=jnp.float32,
    )
    image = direction + back_term.reshape(direction.shape)
    curvature = lax.psum(jnp.sum(direction * image), ("lon", "lat"))
    step_length = old_norm / curvature
    new_residual = residual - step_length * image
    new_norm = lax.psum(jnp.sum(new_residual * new_residual), ("lon", "lat"))
    new_direction = new_residual + new_norm / old_norm * direction
    return (new_residual, new_direction, step_length)


def solution(mesh):
    return jax.shard_map(
        per_device,
        mesh=mesh,
        in_specs=(
            P(None, "lat", "lon"),
            P(None, "lat", "lon"),
            P(),
            P("lat", "lon"),
            P("lat", "lon"),
            P("lat", "lon"),
            P("lat", "lon", None),
            P(None, "lat", "lon", None),
            P(None, "lat", "lon", None),
        ),
        out_specs=(P(None, "lat", "lon"), P(None, "lat", "lon"), P()),
        check_vma=False,
    )
```

profile of v0, /device:TPU:0, one launch (start us, length us, event | category | flops | bytes accessed | tf_op | source)
XLA Modules:
  0.0 281.4 jit_solution(6698378844380854308)
XLA Ops:
  2.6 2.9 %collective-permute-start.1 = (f32[3,8,1]{2,1,0:T(8,128)S(1)}, f32[3,8,1]{2,1,0:T(8,128)S(1)}, u32[]{:S(2)}, u32[]{:S(2)}) collective-permute-start(f32[3,8,1]{2,1,0:T(8,128)S(1)} %get-tuple-element.145), channel_id=1, source_target_pairs={{4,0},{8,4},{12,8},{16,12},{20,16},{24,20},{28,24},{0,28},{5,1},{9... | collective-permute-start | bytes 296 | tf_op jit(solution)/shard_map/ppermute | solution.py:15
  7.2 2.6 collective-permute-start.5
  11.5 2.3 collective-permute-start.2
  13.8 2.1 collective-permute-start.3
  18.3 2.7 collective-permute-done.9
  21.0 1.7 collective-permute-start.10
  22.9 3.8 %collective-permute-start.7 = (f32[75,1,130]{2,0,1:T(8,128)S(1)}, f32[75,1,130]{2,0,1:T(8,128)S(1)}, u32[]{:S(2)}, u32[]{:S(2)}) collective-permute-start(f32[75,1,130]{2,0,1:T(8,128)S(1)} %get-tuple-element.121), channel_id=1, source_target_pairs={{1,0},{2,1},{3,2},{0,3},{5,4},{6,5},{7,6},{4,7},{9,8},{10,9},{11,1... | collective-permute-start | bytes 117008 | tf_op jit(solution)/shard_map/ppermute | solution.py:15
  27.0 2.1 collective-permute-done.6
  31.7 3.3 %collective-permute-done.13 = f32[75,128]{1,0:T(8,128)S(1)} collective-permute-done((f32[75,128]{1,0:T(8,128)S(1)}, f32[75,128]{1,0:T(8,128)S(1)}, u32[]{:S(2)}, u32[]{:S(2)}) %collective-permute-start.13) | collective-permute-done | bytes 38432 | tf_op jit(solution)/shard_map/ppermute | solution.py:21
  35.4 2.6 collective-permute-start.15
  38.0 8.0 %collective-permute-done.14 = f32[75,8,1]{2,0,1:T(8,128)S(1)} collective-permute-done((f32[75,8,1]{2,0,1:T(8,128)S(1)}, f32[75,8,1]{2,0,1:T(8,128)S(1)}, u32[]{:S(2)}, u32[]{:S(2)}) %collective-permute-start.14) | collective-permute-done | bytes 2432 | tf_op jit(solution)/shard_map/ppermute | solution.py:14
  46.3 3.8 %collective-permute-start.17 = (f32[75,1,130]{2,0,1:T(8,128)S(1)}, f32[75,1,130]{2,0,1:T(8,128)S(1)}, u32[]{:S(2)}, u32[]{:S(2)}) collective-permute-start(f32[75,1,130]{2,0,1:T(8,128)S(1)} %get-tuple-element.119), channel_id=1, source_target_pairs={{1,0},{2,1},{3,2},{0,3},{5,4},{6,5},{7,6},{4,7},{9,8},{10,9},{11,1... | collective-permute-start | bytes 117008 | tf_op jit(solution)/shard_map/ppermute | solution.py:15
  50.2 2.3 collective-permute-done.16
  54.6 3.6 %collective-permute-done.20 = f32[75,128]{1,0:T(8,128)S(1)} collective-permute-done((f32[75,128]{1,0:T(8,128)S(1)}, f32[75,128]{1,0:T(8,128)S(1)}, u32[]{:S(2)}, u32[]{:S(2)}) %collective-permute-start.20) | collective-permute-done | bytes 38432 | tf_op jit(solution)/shard_map/ppermute | solution.py:21
  58.5 2.6 collective-permute-start.22
  61.1 7.2 %collective-permute-done.21 = f32[75,8,1]{2,0,1:T(8,128)S(1)} collective-permute-done((f32[75,8,1]{2,0,1:T(8,128)S(1)}, f32[75,8,1]{2,0,1:T(8,128)S(1)}, u32[]{:S(2)}, u32[]{:S(2)}) %collective-permute-start.21) | collective-permute-done | bytes 2432 | tf_op jit(solution)/shard_map/ppermute | solution.py:14
  68.5 3.8 %collective-permute-start.24 = (f32[75,1,130]{2,0,1:T(8,128)S(1)}, f32[75,1,130]{2,0,1:T(8,128)S(1)}, u32[]{:S(2)}, u32[]{:S(2)}) collective-permute-start(f32[75,1,130]{2,0,1:T(8,128)S(1)} %get-tuple-element.117), channel_id=1, source_target_pairs={{1,0},{2,1},{3,2},{0,3},{5,4},{6,5},{7,6},{4,7},{9,8},{10,9},{11,1... | collective-permute-start | bytes 117008 | tf_op jit(solution)/shard_map/ppermute | solution.py:15
  72.4 2.9 %collective-permute-done.23 = f32[75,1,130]{2,0,1:T(8,128)S(1)} collective-permute-done((f32[75,1,130]{2,0,1:T(8,128)S(1)}, f32[75,1,130]{2,0,1:T(8,128)S(1)}, u32[]{:S(2)}, u32[]{:S(2)}) %collective-permute-start.23) | collective-permute-done | bytes 39032 | tf_op jit(solution)/shard_map/ppermute | solution.py:14
  77.2 3.3 %collective-permute-done.27 = f32[75,128]{1,0:T(8,128)S(1)} collective-permute-done((f32[75,128]{1,0:T(8,128)S(1)}, f32[75,128]{1,0:T(8,128)S(1)}, u32[]{:S(2)}, u32[]{:S(2)}) %collective-permute-start.27) | collective-permute-done | bytes 38432 | tf_op jit(solution)/shard_map/ppermute | solution.py:21
  80.8 2.6 collective-permute-start.29
  83.4 7.5 %collective-permute-done.28 = f32[75,8,1]{2,0,1:T(8,128)S(1)} collective-permute-done((f32[75,8,1]{2,0,1:T(8,128)S(1)}, f32[75,8,1]{2,0,1:T(8,128)S(1)}, u32[]{:S(2)}, u32[]{:S(2)}) %collective-permute-start.28) | collective-permute-done | bytes 2432 | tf_op jit(solution)/shard_map/ppermute | solution.py:14
  91.6 3.3 %collective-permute-start.31 = (f32[75,1,130]{2,0,1:T(8,128)S(1)}, f32[75,1,130]{2,0,1:T(8,128)S(1)}, u32[]{:S(2)}, u32[]{:S(2)}) collective-permute-start(f32[75,1,130]{2,0,1:T(8,128)S(1)} %get-tuple-element.115), channel_id=1, source_target_pairs={{1,0},{2,1},{3,2},{0,3},{5,4},{6,5},{7,6},{4,7},{9,8},{10,9},{11,1... | collective-permute-start | bytes 117008 | tf_op jit(solution)/shard_map/ppermute | solution.py:15
  95.2 2.7 collective-permute-done.30
  103.9 2.2 scatter_custom_fusion.1
  106.1 2.4 scatter_custom_fusion.2
  108.6 2.2 scatter_custom_fusion.3
  111.4 3.5 %collective-permute-done.32 = f32[75,9]{0,1:T(8,128)S(1)} collective-permute-done((f32[75,9]{0,1:T(8,128)S(1)}, f32[75,9]{0,1:T(8,128)S(1)}, u32[]{:S(2)}, u32[]{:S(2)}) %collective-permute-start.32) | collective-permute-done | bytes 2732 | tf_op jit(solution)/shard_map/ppermute | solution.py:27
  115.3 3.6 %scatter-add.75 = f32[75,10,130]{2,0,1:T(8,128)S(1)} dynamic-update-slice(f32[75,10,130]{2,0,1:T(8,128)S(1)} %copy.20, f32[75,9,1]{2,0,1:T(8,128)S(1)} %slice_add_fusion, s32[]{:T(128)} %constant.243.clone.1, s32[]{:T(128)} %constant.242.clone.1, s32[]{:T(128)} %constant.242.clone.1) | dynamic-update-slice | bytes 5404 | tf_op jit(solution)/shard_map/scatter-add | solution.py:123
  122.3 2.6 collective-permute-start.35
  124.9 6.8 %collective-permute-done.34 = f32[75,8,1]{2,0,1:T(8,128)S(1)} collective-permute-done((f32[75,8,1]{2,0,1:T(8,128)S(1)}, f32[75,8,1]{2,0,1:T(8,128)S(1)}, u32[]{:S(2)}, u32[]{:S(2)}) %collective-permute-start.34) | collective-permute-done | bytes 2432 | tf_op jit(solution)/shard_map/ppermute | solution.py:14
  131.9 2.5 collective-permute-start.36
  134.4 2.8 collective-permute-start.37
  142.5 1.8 collective-permute-start.40
  144.6 1.9 collective-permute-done.40
  146.8 2.6 collective-permute-start.42
  149.5 7.7 %collective-permute-done.41 = f32[75,8,1]{2,0,1:T(8,128)S(1)} collective-permute-done((f32[75,8,1]{2,0,1:T(8,128)S(1)}, f32[75,8,1]{2,0,1:T(8,128)S(1)}, u32[]{:S(2)}, u32[]{:S(2)}) %collective-permute-start.41) | collective-permute-done | bytes 2432 | tf_op jit(solution)/shard_map/ppermute | solution.py:14
  157.4 3.8 %collective-permute-start.44 = (f32[75,1,130]{2,0,1:T(8,128)S(1)}, f32[75,1,130]{2,0,1:T(8,128)S(1)}, u32[]{:S(2)}, u32[]{:S(2)}) collective-permute-start(f32[75,1,130]{2,0,1:T(8,128)S(1)} %get-tuple-element.111), channel_id=1, source_target_pairs={{1,0},{2,1},{3,2},{0,3},{5,4},{6,5},{7,6},{4,7},{9,8},{10,9},{11,1... | collective-permute-start | bytes 117008 | tf_op jit(solution)/shard_map/ppermute | solution.py:15
  162.4 2.0 collective-permute-done.43
  166.4 1.9 collective-permute-start.47
  168.7 1.7 collective-permute-done.47
  170.8 2.6 collective-permute-start.49
  173.4 7.5 %collective-permute-done.48 = f32[75,8,1]{2,0,1:T(8,128)S(1)} collective-permute-done((f32[75,8,1]{2,0,1:T(8,128)S(1)}, f32[75,8,1]{2,0,1:T(8,128)S(1)}, u32[]{:S(2)}, u32[]{:S(2)}) %collective-permute-start.48) | collective-permute-done | bytes 2432 | tf_op jit(solution)/shard_map/ppermute | solution.py:14
  181.1 3.8 %collective-permute-start.51 = (f32[75,1,130]{2,0,1:T(8,128)S(1)}, f32[75,1,130]{2,0,1:T(8,128)S(1)}, u32[]{:S(2)}, u32[]{:S(2)}) collective-permute-start(f32[75,1,130]{2,0,1:T(8,128)S(1)} %get-tuple-element.109), channel_id=1, source_target_pairs={{1,0},{2,1},{3,2},{0,3},{5,4},{6,5},{7,6},{4,7},{9,8},{10,9},{11,1... | collective-permute-start | bytes 117008 | tf_op jit(solution)/shard_map/ppermute | solution.py:15
  185.6 1.8 collective-permute-done.50
  187.7 1.9 collective-permute-done.53
  191.6 2.1 collective-permute-done.54
  196.1 37.6 %all-reduce = (f32[]{:T(128)}, f32[]{:T(128)}) all-reduce(f32[]{:T(128)} %multiply_reduce_fusion.2, f32[]{:T(128)} %multiply_reduce_fusion.1), channel_id=1, replica_groups=mesh['lon'=8,'lat'=4] {'lon','lat'}, use_global_device_ids=true, to_apply=%region_1.0 | all-reduce | flops 2 | bytes 16 | tf_op jit(solution)/shard_map/psum | solution.py:71
  235.8 42.4 %psum.23 = f32[]{:T(128)} all-reduce(f32[]{:T(128)} %get-tuple-element.102), channel_id=1, replica_groups=mesh['lon'=8,'lat'=4] {'lon','lat'}, use_global_device_ids=true, to_apply=%region_9.11 | all-reduce | flops 1 | bytes 8 | tf_op jit(solution)/shard_map/psum | solution.py:139
  (195 shorter events, 44.4 us)
Async XLA Ops:
  2.1 9.2 %collective-permute-start = (f32[3,8,1]{2,1,0:T(8,128)S(1)}, f32[3,8,1]{2,1,0:T(8,128)S(1)}, u32[]{:S(2)}, u32[]{:S(2)}) collective-permute-start(f32[3,8,1]{2,1,0:T(8,128)S(1)} %get-tuple-element.144), channel_id=1, source_target_pairs={{0,4},{4,8},{8,12},{12,16},{16,20},{20,24},{24,28},{28,0},{1,5},{5... | collective-permute-start | bytes 296 | tf_op jit(solution)/shard_map/ppermute | solution.py:14
  2.6 8.8 %collective-permute-start.1 = (f32[3,8,1]{2,1,0:T(8,128)S(1)}, f32[3,8,1]{2,1,0:T(8,128)S(1)}, u32[]{:S(2)}, u32[]{:S(2)}) collective-permute-start(f32[3,8,1]{2,1,0:T(8,128)S(1)} %get-tuple-element.145), channel_id=1, source_target_pairs={{4,0},{8,4},{12,8},{16,12},{20,16},{24,20},{28,24},{0,28},{5,1},{9... | collective-permute-start | bytes 296 | tf_op jit(solution)/shard_map/ppermute | solution.py:15
  7.1 15.6 %collective-permute-start.4 = (f32[75,8,1]{2,0,1:T(8,128)S(1)}, f32[75,8,1]{2,0,1:T(8,128)S(1)}, u32[]{:S(2)}, u32[]{:S(2)}) collective-permute-start(f32[75,8,1]{2,0,1:T(8,128)S(1)} %get-tuple-element.134), channel_id=1, source_target_pairs={{0,4},{4,8},{8,12},{12,16},{16,20},{20,24},{24,28},{28,0},{1,5},{5... | collective-permute-start | bytes 7208 | tf_op jit(solution)/shard_map/ppermute | solution.py:14
  7.2 15.5 %collective-permute-start.5 = (f32[75,8,1]{2,0,1:T(8,128)S(1)}, f32[75,8,1]{2,0,1:T(8,128)S(1)}, u32[]{:S(2)}, u32[]{:S(2)}) collective-permute-start(f32[75,8,1]{2,0,1:T(8,128)S(1)} %get-tuple-element.135), channel_id=1, source_target_pairs={{4,0},{8,4},{12,8},{16,12},{20,16},{24,20},{28,24},{0,28},{5,1},{9... | collective-permute-start | bytes 7208 | tf_op jit(solution)/shard_map/ppermute | solution.py:15
  9.8 6.1 %collective-permute-start.8 = (f32[2,128]{1,0:T(2,128)S(1)}, f32[2,128]{1,0:T(2,128)S(1)}, u32[]{:S(2)}, u32[]{:S(2)}) collective-permute-start(f32[2,128]{1,0:T(2,128)S(1)} %pad_maximum_fusion.28), channel_id=1, source_target_pairs={{0,4},{4,0},{8,12},{12,8},{16,20},{20,16},{24,28},{28,24},{1,5},{5... | collective-permute-start | bytes 3080 | tf_op jit(solution)/shard_map/ppermute | solution.py:21
  11.5 6.0 %collective-permute-start.2 = (f32[3,1,130]{2,1,0:T(1,128)S(1)}, f32[3,1,130]{2,1,0:T(1,128)S(1)}, u32[]{:S(2)}, u32[]{:S(2)}) collective-permute-start(f32[3,1,130]{2,1,0:T(1,128)S(1)} %get-tuple-element.138), channel_id=1, source_target_pairs={{0,1},{1,2},{2,3},{3,0},{4,5},{5,6},{6,7},{7,4},{8,9},{9,10},{10,1... | collective-permute-start | bytes 4688 | tf_op jit(solution)/shard_map/ppermute | solution.py:14
  13.8 4.3 %collective-permute-start.3 = (f32[3,1,130]{2,1,0:T(1,128)S(1)}, f32[3,1,130]{2,1,0:T(1,128)S(1)}, u32[]{:S(2)}, u32[]{:S(2)}) collective-permute-start(f32[3,1,130]{2,1,0:T(1,128)S(1)} %get-tuple-element.139), channel_id=1, source_target_pairs={{1,0},{2,1},{3,2},{0,3},{5,4},{6,5},{7,6},{4,7},{9,8},{10,9},{11,1... | collective-permute-start | bytes 4688 | tf_op jit(solution)/shard_map/ppermute | solution.py:15
  15.9 11.0 %collective-permute-start.11 = (f32[75,128]{1,0:T(8,128)S(1)}, f32[75,128]{1,0:T(8,128)S(1)}, u32[]{:S(2)}, u32[]{:S(2)}) collective-permute-start(f32[75,128]{1,0:T(8,128)S(1)} %slice_bitcast_fusion.7), channel_id=1, source_target_pairs={{0,4},{4,0},{8,12},{12,8},{16,20},{20,16},{24,28},{28,24},{1,5},{5... | collective-permute-start | bytes 115208 | tf_op jit(solution)/shard_map/ppermute | solution.py:21
  21.0 5.7 %collective-permute-start.10 = (f32[2,128]{1,0:T(2,128)S(1)}, f32[2,128]{1,0:T(2,128)S(1)}, u32[]{:S(2)}, u32[]{:S(2)}) collective-permute-start(f32[2,128]{1,0:T(2,128)S(1)} %collective-permute-done.9), channel_id=1, source_target_pairs={{0,16},{4,20},{8,24},{12,28},{16,0},{20,4},{24,8},{28,12},{1,17},{... | collective-permute-start | bytes 3080 | tf_op jit(solution)/shard_map/ppermute | solution.py:21
  22.9 6.3 %collective-permute-start.6 = (f32[75,1,130]{2,0,1:T(8,128)S(1)}, f32[75,1,130]{2,0,1:T(8,128)S(1)}, u32[]{:S(2)}, u32[]{:S(2)}) collective-permute-start(f32[75,1,130]{2,0,1:T(8,128)S(1)} %get-tuple-element.120), channel_id=1, source_target_pairs={{0,1},{1,2},{2,3},{3,0},{4,5},{5,6},{6,7},{7,4},{8,9},{9,10},{10,1... | collective-permute-start | bytes 117008 | tf_op jit(solution)/shard_map/ppermute | solution.py:14
  22.9 6.2 %collective-permute-start.7 = (f32[75,1,130]{2,0,1:T(8,128)S(1)}, f32[75,1,130]{2,0,1:T(8,128)S(1)}, u32[]{:S(2)}, u32[]{:S(2)}) collective-permute-start(f32[75,1,130]{2,0,1:T(8,128)S(1)} %get-tuple-element.121), channel_id=1, source_target_pairs={{1,0},{2,1},{3,2},{0,3},{5,4},{6,5},{7,6},{4,7},{9,8},{10,9},{11,1... | collective-permute-start | bytes 117008 | tf_op jit(solution)/shard_map/ppermute | solution.py:15
  26.9 4.1 %collective-permute-start.12 = (f32[75,128]{1,0:T(8,128)S(1)}, f32[75,128]{1,0:T(8,128)S(1)}, u32[]{:S(2)}, u32[]{:S(2)}) collective-permute-start(f32[75,128]{1,0:T(8,128)S(1)} %collective-permute-done.11), channel_id=1, source_target_pairs={{0,8},{4,12},{8,0},{12,4},{16,24},{20,28},{24,16},{28,20},{1,9},{5... | collective-permute-start | bytes 115208 | tf_op jit(solution)/shard_map/ppermute | solution.py:21
  31.0 4.0 %collective-permute-start.13 = (f32[75,128]{1,0:T(8,128)S(1)}, f32[75,128]{1,0:T(8,128)S(1)}, u32[]{:S(2)}, u32[]{:S(2)}) collective-permute-start(f32[75,128]{1,0:T(8,128)S(1)} %collective-permute-done.12), channel_id=1, source_target_pairs={{0,16},{4,20},{8,24},{12,28},{16,0},{20,4},{24,8},{28,12},{1,17},{... | collective-permute-start | bytes 115208 | tf_op jit(solution)/shard_map/ppermute | solution.py:21
  35.3 10.7 %collective-permute-start.14 = (f32[75,8,1]{2,0,1:T(8,128)S(1)}, f32[75,8,1]{2,0,1:T(8,128)S(1)}, u32[]{:S(2)}, u32[]{:S(2)}) collective-permute-start(f32[75,8,1]{2,0,1:T(8,128)S(1)} %get-tuple-element.132), channel_id=1, source_target_pairs={{0,4},{4,8},{8,12},{12,16},{16,20},{20,24},{24,28},{28,0},{1,5},{5... | collective-permute-start | bytes 7208 | tf_op jit(solution)/shard_map/ppermute | solution.py:14
  35.4 10.7 %collective-permute-start.15 = (f32[75,8,1]{2,0,1:T(8,128)S(1)}, f32[75,8,1]{2,0,1:T(8,128)S(1)}, u32[]{:S(2)}, u32[]{:S(2)}) collective-permute-start(f32[75,8,1]{2,0,1:T(8,128)S(1)} %get-tuple-element.133), channel_id=1, source_target_pairs={{4,0},{8,4},{12,8},{16,12},{20,16},{24,20},{28,24},{0,28},{5,1},{9... | collective-permute-start | bytes 7208 | tf_op jit(solution)/shard_map/ppermute | solution.py:15
  38.0 12.1 %collective-permute-start.18 = (f32[75,128]{1,0:T(8,128)S(1)}, f32[75,128]{1,0:T(8,128)S(1)}, u32[]{:S(2)}, u32[]{:S(2)}) collective-permute-start(f32[75,128]{1,0:T(8,128)S(1)} %slice_bitcast_fusion.6), channel_id=1, source_target_pairs={{0,4},{4,0},{8,12},{12,8},{16,20},{20,16},{24,28},{28,24},{1,5},{5... | collective-permute-start | bytes 115208 | tf_op jit(solution)/shard_map/ppermute | solution.py:21
  46.2 6.3 %collective-permute-start.16 = (f32[75,1,130]{2,0,1:T(8,128)S(1)}, f32[75,1,130]{2,0,1:T(8,128)S(1)}, u32[]{:S(2)}, u32[]{:S(2)}) collective-permute-start(f32[75,1,130]{2,0,1:T(8,128)S(1)} %get-tuple-element.118), channel_id=1, source_target_pairs={{0,1},{1,2},{2,3},{3,0},{4,5},{5,6},{6,7},{7,4},{8,9},{9,10},{10,1... | collective-permute-start | bytes 117008 | tf_op jit(solution)/shard_map/ppermute | solution.py:14
  46.3 6.2 %collective-permute-start.17 = (f32[75,1,130]{2,0,1:T(8,128)S(1)}, f32[75,1,130]{2,0,1:T(8,128)S(1)}, u32[]{:S(2)}, u32[]{:S(2)}) collective-permute-start(f32[75,1,130]{2,0,1:T(8,128)S(1)} %get-tuple-element.119), channel_id=1, source_target_pairs={{1,0},{2,1},{3,2},{0,3},{5,4},{6,5},{7,6},{4,7},{9,8},{10,9},{11,1... | collective-permute-start | bytes 117008 | tf_op jit(solution)/shard_map/ppermute | solution.py:15
  50.1 4.1 %collective-permute-start.19 = (f32[75,128]{1,0:T(8,128)S(1)}, f32[75,128]{1,0:T(8,128)S(1)}, u32[]{:S(2)}, u32[]{:S(2)}) collective-permute-start(f32[75,128]{1,0:T(8,128)S(1)} %collective-permute-done.18), channel_id=1, source_target_pairs={{0,8},{4,12},{8,0},{12,4},{16,24},{20,28},{24,16},{28,20},{1,9},{5... | collective-permute-start | bytes 115208 | tf_op jit(solution)/shard_map/ppermute | solution.py:21
  54.1 4.0 %collective-permute-start.20 = (f32[75,128]{1,0:T(8,128)S(1)}, f32[75,128]{1,0:T(8,128)S(1)}, u32[]{:S(2)}, u32[]{:S(2)}) collective-permute-start(f32[75,128]{1,0:T(8,128)S(1)} %collective-permute-done.19), channel_id=1, source_target_pairs={{0,16},{4,20},{8,24},{12,28},{16,0},{20,4},{24,8},{28,12},{1,17},{... | collective-permute-start | bytes 115208 | tf_op jit(solution)/shard_map/ppermute | solution.py:21
  58.4 9.9 %collective-permute-start.21 = (f32[75,8,1]{2,0,1:T(8,128)S(1)}, f32[75,8,1]{2,0,1:T(8,128)S(1)}, u32[]{:S(2)}, u32[]{:S(2)}) collective-permute-start(f32[75,8,1]{2,0,1:T(8,128)S(1)} %get-tuple-element.130), channel_id=1, source_target_pairs={{0,4},{4,8},{8,12},{12,16},{16,20},{20,24},{24,28},{28,0},{1,5},{5... | collective-permute-start | bytes 7208 | tf_op jit(solution)/shard_map/ppermute | solution.py:14
  58.5 9.8 %collective-permute-start.22 = (f32[75,8,1]{2,0,1:T(8,128)S(1)}, f32[75,8,1]{2,0,1:T(8,128)S(1)}, u32[]{:S(2)}, u32[]{:S(2)}) collective-permute-start(f32[75,8,1]{2,0,1:T(8,128)S(1)} %get-tuple-element.131), channel_id=1, source_target_pairs={{4,0},{8,4},{12,8},{16,12},{20,16},{24,20},{28,24},{0,28},{5,1},{9... | collective-permute-start | bytes 7208 | tf_op jit(solution)/shard_map/ppermute | solution.py:15
  61.1 11.2 %collective-permute-start.25 = (f32[75,128]{1,0:T(8,128)S(1)}, f32[75,128]{1,0:T(8,128)S(1)}, u32[]{:S(2)}, u32[]{:S(2)}) collective-permute-start(f32[75,128]{1,0:T(8,128)S(1)} %slice_bitcast_fusion.5), channel_id=1, source_target_pairs={{0,4},{4,0},{8,12},{12,8},{16,20},{20,16},{24,28},{28,24},{1,5},{5... | collective-permute-start | bytes 115208 | tf_op jit(solution)/shard_map/ppermute | solution.py:21
  68.4 6.9 %collective-permute-start.23 = (f32[75,1,130]{2,0,1:T(8,128)S(1)}, f32[75,1,130]{2,0,1:T(8,128)S(1)}, u32[]{:S(2)}, u32[]{:S(2)}) collective-permute-start(f32[75,1,130]{2,0,1:T(8,128)S(1)} %get-tuple-element.116), channel_id=1, source_target_pairs={{0,1},{1,2},{2,3},{3,0},{4,5},{5,6},{6,7},{7,4},{8,9},{9,10},{10,1... | collective-permute-start | bytes 117008 | tf_op jit(solution)/shard_map/ppermute | solution.py:14
  68.5 6.9 %collective-permute-start.24 = (f32[75,1,130]{2,0,1:T(8,128)S(1)}, f32[75,1,130]{2,0,1:T(8,128)S(1)}, u32[]{:S(2)}, u32[]{:S(2)}) collective-permute-start(f32[75,1,130]{2,0,1:T(8,128)S(1)} %get-tuple-element.117), channel_id=1, source_target_pairs={{1,0},{2,1},{3,2},{0,3},{5,4},{6,5},{7,6},{4,7},{9,8},{10,9},{11,1... | collective-permute-start | bytes 117008 | tf_op jit(solution)/shard_map/ppermute | solution.py:15
  72.3 4.1 %collective-permute-start.26 = (f32[75,128]{1,0:T(8,128)S(1)}, f32[75,128]{1,0:T(8,128)S(1)}, u32[]{:S(2)}, u32[]{:S(2)}) collective-permute-start(f32[75,128]{1,0:T(8,128)S(1)} %collective-permute-done.25), channel_id=1, source_target_pairs={{0,8},{4,12},{8,0},{12,4},{16,24},{20,28},{24,16},{28,20},{1,9},{5... | collective-permute-start | bytes 115208 | tf_op jit(solution)/shard_map/ppermute | solution.py:21
  76.4 4.0 %collective-permute-start.27 = (f32[75,128]{1,0:T(8,128)S(1)}, f32[75,128]{1,0:T(8,128)S(1)}, u32[]{:S(2)}, u32[]{:S(2)}) collective-permute-start(f32[75,128]{1,0:T(8,128)S(1)} %collective-permute-done.26), channel_id=1, source_target_pairs={{0,16},{4,20},{8,24},{12,28},{16,0},{20,4},{24,8},{28,12},{1,17},{... | collective-permute-start | bytes 115208 | tf_op jit(solution)/shard_map/ppermute | solution.py:21
  80.7 10.2 %collective-permute-start.28 = (f32[75,8,1]{2,0,1:T(8,128)S(1)}, f32[75,8,1]{2,0,1:T(8,128)S(1)}, u32[]{:S(2)}, u32[]{:S(2)}) collective-permute-start(f32[75,8,1]{2,0,1:T(8,128)S(1)} %get-tuple-element.128), channel_id=1, source_target_pairs={{0,4},{4,8},{8,12},{12,16},{16,20},{20,24},{24,28},{28,0},{1,5},{5... | collective-permute-start | bytes 7208 | tf_op jit(solution)/shard_map/ppermute | solution.py:14
  80.8 10.1 %collective-permute-start.29 = (f32[75,8,1]{2,0,1:T(8,128)S(1)}, f32[75,8,1]{2,0,1:T(8,128)S(1)}, u32[]{:S(2)}, u32[]{:S(2)}) collective-permute-start(f32[75,8,1]{2,0,1:T(8,128)S(1)} %get-tuple-element.129), channel_id=1, source_target_pairs={{4,0},{8,4},{12,8},{16,12},{20,16},{24,20},{28,24},{0,28},{5,1},{9... | collective-permute-start | bytes 7208 | tf_op jit(solution)/shard_map/ppermute | solution.py:15
  91.0 6.9 %collective-permute-start.30 = (f32[75,1,130]{2,0,1:T(8,128)S(1)}, f32[75,1,130]{2,0,1:T(8,128)S(1)}, u32[]{:S(2)}, u32[]{:S(2)}) collective-permute-start(f32[75,1,130]{2,0,1:T(8,128)S(1)} %get-tuple-element.114), channel_id=1, source_target_pairs={{0,1},{1,2},{2,3},{3,0},{4,5},{5,6},{6,7},{7,4},{8,9},{9,10},{10,1... | collective-permute-start | bytes 117008 | tf_op jit(solution)/shard_map/ppermute | solution.py:14
  91.6 6.3 %collective-permute-start.31 = (f32[75,1,130]{2,0,1:T(8,128)S(1)}, f32[75,1,130]{2,0,1:T(8,128)S(1)}, u32[]{:S(2)}, u32[]{:S(2)}) collective-permute-start(f32[75,1,130]{2,0,1:T(8,128)S(1)} %get-tuple-element.115), channel_id=1, source_target_pairs={{1,0},{2,1},{3,2},{0,3},{5,4},{6,5},{7,6},{4,7},{9,8},{10,9},{11,1... | collective-permute-start | bytes 117008 | tf_op jit(solution)/shard_map/ppermute | solution.py:15
  110.9 4.0 %collective-permute-start.32 = (f32[75,9]{0,1:T(8,128)S(1)}, f32[75,9]{0,1:T(8,128)S(1)}, u32[]{:S(2)}, u32[]{:S(2)}) collective-permute-start(f32[75,9]{0,1:T(8,128)S(1)} %bitcast.153), channel_id=1, source_target_pairs={{0,4},{4,8},{8,12},{12,16},{16,20},{20,24},{24,28},{28,0},{1,5},{5... | collective-permute-start | bytes 8108 | tf_op jit(solution)/shard_map/ppermute | solution.py:27
  122.2 9.5 %collective-permute-start.34 = (f32[75,8,1]{2,0,1:T(8,128)S(1)}, f32[75,8,1]{2,0,1:T(8,128)S(1)}, u32[]{:S(2)}, u32[]{:S(2)}) collective-permute-start(f32[75,8,1]{2,0,1:T(8,128)S(1)} %get-tuple-element.126), channel_id=1, source_target_pairs={{0,4},{4,8},{8,12},{12,16},{16,20},{20,24},{24,28},{28,0},{1,5},{5... | collective-permute-start | bytes 7208 | tf_op jit(solution)/shard_map/ppermute | solution.py:14
  122.3 9.4 %collective-permute-start.35 = (f32[75,8,1]{2,0,1:T(8,128)S(1)}, f32[75,8,1]{2,0,1:T(8,128)S(1)}, u32[]{:S(2)}, u32[]{:S(2)}) collective-permute-start(f32[75,8,1]{2,0,1:T(8,128)S(1)} %get-tuple-element.127), channel_id=1, source_target_pairs={{4,0},{8,4},{12,8},{16,12},{20,16},{24,20},{28,24},{0,28},{5,1},{9... | collective-permute-start | bytes 7208 | tf_op jit(solution)/shard_map/ppermute | solution.py:15
  131.9 8.6 %collective-permute-start.36 = (f32[75,1,130]{2,0,1:T(8,128)S(1)}, f32[75,1,130]{2,0,1:T(8,128)S(1)}, u32[]{:S(2)}, u32[]{:S(2)}) collective-permute-start(f32[75,1,130]{2,0,1:T(8,128)S(1)} %get-tuple-element.112), channel_id=1, source_target_pairs={{0,1},{1,2},{2,3},{3,0},{4,5},{5,6},{6,7},{7,4},{8,9},{9,10},{10,1... | collective-permute-start | bytes 117008 | tf_op jit(solution)/shard_map/ppermute | solution.py:14
  134.4 6.0 %collective-permute-start.37 = (f32[75,1,130]{2,0,1:T(8,128)S(1)}, f32[75,1,130]{2,0,1:T(8,128)S(1)}, u32[]{:S(2)}, u32[]{:S(2)}) collective-permute-start(f32[75,1,130]{2,0,1:T(8,128)S(1)} %get-tuple-element.113), channel_id=1, source_target_pairs={{1,0},{2,1},{3,2},{0,3},{5,4},{6,5},{7,6},{4,7},{9,8},{10,9},{11,1... | collective-permute-start | bytes 117008 | tf_op jit(solution)/shard_map/ppermute | solution.py:15
  146.8 10.4 %collective-permute-start.41 = (f32[75,8,1]{2,0,1:T(8,128)S(1)}, f32[75,8,1]{2,0,1:T(8,128)S(1)}, u32[]{:S(2)}, u32[]{:S(2)}) collective-permute-start(f32[75,8,1]{2,0,1:T(8,128)S(1)} %get-tuple-element.124), channel_id=1, source_target_pairs={{0,4},{4,8},{8,12},{12,16},{16,20},{20,24},{24,28},{28,0},{1,5},{5... | collective-permute-start | bytes 7208 | tf_op jit(solution)/shard_map/ppermute | solution.py:14
  146.8 10.3 %collective-permute-start.42 = (f32[75,8,1]{2,0,1:T(8,128)S(1)}, f32[75,8,1]{2,0,1:T(8,128)S(1)}, u32[]{:S(2)}, u32[]{:S(2)}) collective-permute-start(f32[75,8,1]{2,0,1:T(8,128)S(1)} %get-tuple-element.125), channel_id=1, source_target_pairs={{4,0},{8,4},{12,8},{16,12},{20,16},{24,20},{28,24},{0,28},{5,1},{9... | collective-permute-start | bytes 7208 | tf_op jit(solution)/shard_map/ppermute | solution.py:15
  157.3 7.1 %collective-permute-start.43 = (f32[75,1,130]{2,0,1:T(8,128)S(1)}, f32[75,1,130]{2,0,1:T(8,128)S(1)}, u32[]{:S(2)}, u32[]{:S(2)}) collective-permute-start(f32[75,1,130]{2,0,1:T(8,128)S(1)} %get-tuple-element.110), channel_id=1, source_target_pairs={{0,1},{1,2},{2,3},{3,0},{4,5},{5,6},{6,7},{7,4},{8,9},{9,10},{10,1... | collective-permute-start | bytes 117008 | tf_op jit(solution)/shard_map/ppermute | solution.py:14
  157.4 7.1 %collective-permute-start.44 = (f32[75,1,130]{2,0,1:T(8,128)S(1)}, f32[75,1,130]{2,0,1:T(8,128)S(1)}, u32[]{:S(2)}, u32[]{:S(2)}) collective-permute-start(f32[75,1,130]{2,0,1:T(8,128)S(1)} %get-tuple-element.111), channel_id=1, source_target_pairs={{1,0},{2,1},{3,2},{0,3},{5,4},{6,5},{7,6},{4,7},{9,8},{10,9},{11,1... | collective-permute-start | bytes 117008 | tf_op jit(solution)/shard_map/ppermute | solution.py:15
  162.4 4.0 %collective-permute-start.46 = (f32[75,128]{1,0:T(8,128)S(1)}, f32[75,128]{1,0:T(8,128)S(1)}, u32[]{:S(2)}, u32[]{:S(2)}) collective-permute-start(f32[75,128]{1,0:T(8,128)S(1)} %collective-permute-done.45), channel_id=1, source_target_pairs={{0,8},{4,12},{8,0},{12,4},{16,24},{20,28},{24,16},{28,20},{1,9},{5... | collective-permute-start | bytes 115208 | tf_op jit(solution)/shard_map/ppermute | solution.py:21
  170.7 10.2 %collective-permute-start.48 = (f32[75,8,1]{2,0,1:T(8,128)S(1)}, f32[75,8,1]{2,0,1:T(8,128)S(1)}, u32[]{:S(2)}, u32[]{:S(2)}) collective-permute-start(f32[75,8,1]{2,0,1:T(8,128)S(1)} %get-tuple-element.122), channel_id=1, source_target_pairs={{0,4},{4,8},{8,12},{12,16},{16,20},{20,24},{24,28},{28,0},{1,5},{5... | collective-permute-start | bytes 7208 | tf_op jit(solution)/shard_map/ppermute | solution.py:14
  170.8 10.2 %collective-permute-start.49 = (f32[75,8,1]{2,0,1:T(8,128)S(1)}, f32[75,8,1]{2,0,1:T(8,128)S(1)}, u32[]{:S(2)}, u32[]{:S(2)}) collective-permute-start(f32[75,8,1]{2,0,1:T(8,128)S(1)} %get-tuple-element.123), channel_id=1, source_target_pairs={{4,0},{8,4},{12,8},{16,12},{20,16},{24,20},{28,24},{0,28},{5,1},{9... | collective-permute-start | bytes 7208 | tf_op jit(solution)/shard_map/ppermute | solution.py:15
  173.4 12.2 %collective-permute-start.52 = (f32[75,128]{1,0:T(8,128)S(1)}, f32[75,128]{1,0:T(8,128)S(1)}, u32[]{:S(2)}, u32[]{:S(2)}) collective-permute-start(f32[75,128]{1,0:T(8,128)S(1)} %slice_bitcast_fusion.1), channel_id=1, source_target_pairs={{0,4},{4,0},{8,12},{12,8},{16,20},{20,16},{24,28},{28,24},{1,5},{5... | collective-permute-start | bytes 115208 | tf_op jit(solution)/shard_map/ppermute | solution.py:21
  181.1 6.3 %collective-permute-start.50 = (f32[75,1,130]{2,0,1:T(8,128)S(1)}, f32[75,1,130]{2,0,1:T(8,128)S(1)}, u32[]{:S(2)}, u32[]{:S(2)}) collective-permute-start(f32[75,1,130]{2,0,1:T(8,128)S(1)} %get-tuple-element.108), channel_id=1, source_target_pairs={{0,1},{1,2},{2,3},{3,0},{4,5},{5,6},{6,7},{7,4},{8,9},{9,10},{10,1... | collective-permute-start | bytes 117008 | tf_op jit(solution)/shard_map/ppermute | solution.py:14
  181.1 6.3 %collective-permute-start.51 = (f32[75,1,130]{2,0,1:T(8,128)S(1)}, f32[75,1,130]{2,0,1:T(8,128)S(1)}, u32[]{:S(2)}, u32[]{:S(2)}) collective-permute-start(f32[75,1,130]{2,0,1:T(8,128)S(1)} %get-tuple-element.109), channel_id=1, source_target_pairs={{1,0},{2,1},{3,2},{0,3},{5,4},{6,5},{7,6},{4,7},{9,8},{10,9},{11,1... | collective-permute-start | bytes 117008 | tf_op jit(solution)/shard_map/ppermute | solution.py:15
  185.6 4.0 %collective-permute-start.53 = (f32[75,128]{1,0:T(8,128)S(1)}, f32[75,128]{1,0:T(8,128)S(1)}, u32[]{:S(2)}, u32[]{:S(2)}) collective-permute-start(f32[75,128]{1,0:T(8,128)S(1)} %collective-permute-done.52), channel_id=1, source_target_pairs={{0,8},{4,12},{8,0},{12,4},{16,24},{20,28},{24,16},{28,20},{1,9},{5... | collective-permute-start | bytes 115208 | tf_op jit(solution)/shard_map/ppermute | solution.py:21
  189.6 4.0 %collective-permute-start.54 = (f32[75,128]{1,0:T(8,128)S(1)}, f32[75,128]{1,0:T(8,128)S(1)}, u32[]{:S(2)}, u32[]{:S(2)}) collective-permute-start(f32[75,128]{1,0:T(8,128)S(1)} %collective-permute-done.53), channel_id=1, source_target_pairs={{0,16},{4,20},{8,24},{12,28},{16,0},{20,4},{24,8},{28,12},{1,17},{... | collective-permute-start | bytes 115208 | tf_op jit(solution)/shard_map/ppermute | solution.py:21
  (16 other events, 90.9 us)
where the time goes:
time: 282 us; the launch traced here: 281 us
  waiting for transfers between devices  96 us (34%)
  blocking collectives  80 us (28%)
  starting transfers between devices  66.1 us (23%)
  other arithmetic  18.9 us (7%)
  local copies, waits for them, and re-layouts  14.2 us (5%)
  between operations  5.25 us (2%)
    ppermute x16, waiting for transfers between devices, padded_2(): before = lax.ppermute(last, axis, up)  61.4 us
    ppermute x16, starting transfers between devices, padded_2(): after = lax.ppermute(leading, axis, down)  48.6 us
    psum x1, blocking collectives, per_device(): new_norm = lax.psum(jnp.sum(new_residual * new_residual), ('lon', 'lat'))  42.4 us
    psum x1, blocking collectives, per_device(): old_norm = lax.psum(jnp.sum(residual * residual), ('lon', 'lat'))  37.6 us
    ppermute x21, waiting for transfers between devices, swapped(): lax.ppermute(array, axis, [(i, i ^ 1 << stride) for i in range(lax.axis_s...  29.6 us
    ppermute x21, starting transfers between devices, swapped(): lax.ppermute(array, axis, [(i, i ^ 1 << stride) for i in range(lax.axis_s...  9.47 us
    scatter-add x4, other arithmetic, per_device(): spread.at[:, corner_index[corner]]  8.57 us
    ppermute x16, starting transfers between devices, padded_2(): before = lax.ppermute(last, axis, up)  6.61 us
  transfers between devices with their start and end apart: 55, of which 31 were waited for; matrix products, arithmetic and copies ran while one was open for 3% of the time, Pallas kernels for 0%

commit v1 on v0

v1 whole, which is shorter than its diff:
```python
import jax
import jax.numpy as jnp
from jax import lax
from jax.experimental import pallas as pl
from jax.experimental.pallas import tpu as pltpu
from jax.sharding import PartitionSpec as P

F32 = jnp.float32
MESH = pl.DeviceIdType.MESH


def mm(a, b, dims=((1,), (0,))):
    return lax.dot_general(
        a, b, (dims, ((), ())), precision=lax.Precision.HIGHEST, preferred_element_type=F32
    )


def make_kernel(n_lon, n_lat, levels, rows, width, n_obs):
    padded_levels = -(-(levels + 3) // 8) * 8
    lp = padded_levels
    ke_at, kn_at, wet_at = levels, levels + 1, levels + 2
    first = 4
    top_slot = first + rows - 1
    after = first + rows

    def roll(x, shift):
        shift = shift % width
        return x if shift == 0 else pltpu.roll(x, shift, 1)

    def kernel(
        d_ref, r_ref, eof_ref, ke_ref, kn_ref, wet_ref, base_ref, frac_ref, rinv_ref,
        nr_ref, nd_ref, step_ref,
        field_a, field_b, halo_a, halo_b, coef, hcoef,
        pack_a, east_a, west_a, comb_a, flip_a, flipc_a, north_a, south_a, cnorth_a, csouth_a,
        spread, pack_b, east_b, west_b, comb_b, flip_b, flipc_b, north_b, south_b, cnorth_b, csouth_b,
        eof_pad, rinv_pad, image, red, lon_in, red2, lat_in,
        send_sem, recv_sem, lon_send, lon_recv, lat_send, lat_recv,
    ):
        lon = lax.axis_index("lon")
        lat = lax.axis_index("lat")
        is_top = lat == n_lat - 1
        is_bottom = lat == 0
        east = (lax.rem(lon + 1, n_lon), lat)
        west = (lax.rem(lon + n_lon - 1, n_lon), lat)
        mirror = (n_lon - 1 - lon, lat)
        north = (lon, lax.rem(lat + 1, n_lat))
        south = (lon, lax.rem(lat + n_lat - 1, n_lat))
        lane = lax.broadcasted_iota(jnp.int32, (lp, width), 1)
        lane1 = lane[:1]
        sub8 = lax.rem(lane, 8)

        barrier = pltpu.get_barrier_semaphore()
        for k in range(1, n_lon):
            pl.semaphore_signal(barrier, inc=1, device_id=(lax.rem(lon + k, n_lon), lat), device_id_type=MESH)
        for k in range(1, n_lat):
            pl.semaphore_signal(barrier, inc=1, device_id=(lon, lax.rem(lat + k, n_lat)), device_id_type=MESH)

        for j in range(rows):
            e = first + j
            field_a[e, 0:levels, :] = d_ref[:, j, :]
            field_a[e, ke_at : ke_at + 1, :] = ke_ref[j : j + 1, :]
            field_a[e, kn_at : kn_at + 1, :] = kn_ref[j : j + 1, :]
            field_a[e, wet_at : wet_at + 1, :] = wet_ref[j : j + 1, :].astype(F32)
            if lp > levels + 3:
                field_a[e, levels + 3 : lp, :] = jnp.zeros((lp - levels - 3, width), F32)

        def group(e):
            off = lane - e * 8
            return (off >= -4) & (off < 4)

        def packed(ref, slots, shift=0):
            out = jnp.zeros((lp, width), F32)
            for e in slots:
                out = jnp.where(group(e), roll(ref[e - shift], e * 8), out)
            return out

        row_id = lax.broadcasted_iota(jnp.int32, (width, width), 0)
        col_id = lax.broadcasted_iota(jnp.int32, (width, width), 1)
        reverse = (row_id + col_id == width - 1).astype(F32)

        def flip(x):
            return mm(x, reverse)

        def flip_packed(x):
            return roll(mm(x, reverse), (2 * top_slot + 1) * 8 - 64 - width)

        def remote(src, dst, index, device):
            return pltpu.make_async_remote_copy(
                src_ref=src, dst_ref=dst, send_sem=send_sem.at[index], recv_sem=recv_sem.at[index],
                device_id=device, device_id_type=MESH,
            )

        pack_a[...] = packed(field_a, range(first, after))
        pl.semaphore_wait(barrier, n_lon + n_lat - 2)

        to_west = remote(pack_a, east_a, 0, west)
        to_east = remote(pack_a, west_a, 1, east)
        to_west.start()
        to_east.start()
        to_north = remote(field_a.at[pl.ds(after - 3, 3)], south_a, 2, north)
        to_south = remote(field_a.at[pl.ds(first, 4)], north_a, 3, south)

        @pl.when(jnp.logical_not(is_top))
        def _():
            to_north.start()

        @pl.when(jnp.logical_not(is_bottom))
        def _():
            to_south.start()

        @pl.when(is_top)
        def _():
            for k in range(4):
                flip_a[k] = flip(field_a[top_slot - k])
            pltpu.make_async_remote_copy(
                src_ref=flip_a, dst_ref=north_a, send_sem=send_sem.at[2], recv_sem=recv_sem.at[3],
                device_id=mirror, device_id_type=MESH,
            ).start()

        base = base_ref[...]
        lat_frac = frac_ref[0:1, :]
        lon_frac = frac_ref[1:2, :]
        base_row = jnp.zeros_like(base)
        for j in range(1, rows):
            base_row = base_row + (base >= j * width).astype(jnp.int32)
        base_col = base - base_row * width
        zero_obs = jnp.zeros((1, n_obs), F32)

        def row_weight(j):
            return jnp.where(base_row == j, 1.0 - lat_frac, zero_obs) + jnp.where(
                base_row + 1 == j, lat_frac, zero_obs
            )

        row_weights = [row_weight(j) for j in range(rows + 1)]
        cell = lax.broadcasted_iota(jnp.int32, (width, n_obs), 0)
        col_weight = jnp.where(cell == base_col, 1.0 - lon_frac, 0.0) + jnp.where(
            cell == base_col + 1, lon_frac, 0.0
        )
        last_weight = jnp.where(base_col == width - 1, lon_frac, zero_obs)
        rim_low = (first + base_row) * 8
        rim_weight = jnp.where(cell == rim_low, (1.0 - lat_frac) * last_weight, 0.0) + jnp.where(
            cell == rim_low + 8, lat_frac * last_weight, 0.0
        )
        eof_pad[...] = jnp.zeros_like(eof_pad)
        eof_pad[0:levels, 0:levels] = eof_ref[...]
        rinv_pad[levels - levels % 8 : lp, :] = jnp.zeros((lp - (levels - levels % 8), n_obs), F32)
        rinv_pad[0:levels, :] = rinv_ref[...]
        eof_full = eof_pad[...]
        eof = eof_full[:lp, :lp]
        eof_t = eof_full.T[:lp, :lp]

        def second_leg(comb, flipc, cnorth, csouth, start):
            legs = (
                remote(comb, csouth, start, north),
                remote(comb, cnorth, start + 1, south),
                pltpu.make_async_remote_copy(
                    src_ref=flipc, dst_ref=cnorth, send_sem=send_sem.at[start],
                    recv_sem=recv_sem.at[start + 1], device_id=mirror, device_id_type=MESH,
                ),
            )

            @pl.when(jnp.logical_not(is_top))
            def _():
                legs[0].start()

            @pl.when(jnp.logical_not(is_bottom))
            def _():
                legs[1].start()

            @pl.when(is_top)
            def _():
                flipc[...] = flip_packed(comb[...])
                legs[2].start()

            return legs

        to_west.wait_recv()
        to_east.wait_recv()
        comb_a[...] = jnp.where(sub8 < 4, east_a[...], west_a[...])
        legs_a = second_leg(comb_a, flipc_a, cnorth_a, csouth_a, 4)

        @pl.when(is_bottom)
        def _():
            south_a[...] = jnp.zeros_like(south_a)
            csouth_a[...] = jnp.zeros_like(csouth_a)

        to_south.wait_recv()

        @pl.when(jnp.logical_not(is_bottom))
        def _():
            to_north.wait_recv()

        for k in range(4):
            field_a[after + k] = north_a[k]
        for k in range(3):
            field_a[first - 3 + k] = south_a[k]
        legs_a[1].wait_recv()

        @pl.when(jnp.logical_not(is_bottom))
        def _():
            legs_a[0].wait_recv()

        in_north = (lane >= after * 8 - 4) & (lane < (after + 4) * 8 - 4)
        in_south = (lane < first * 8 - 4) | (lane >= (after + 4) * 8 - 4)
        halo_a[...] = jnp.where(
            in_north, roll(cnorth_a[...], 64), jnp.where(in_south, roll(csouth_a[...], 64), comb_a[...])
        )

        low, high = first - 3, after + 3

        def shifted_rim(h, crossing):
            he = roll(jnp.where(lax.rem(lane[: h.shape[0]], 8) == 0, crossing, h), -1)
            hw = roll(jnp.where(lax.rem(lane[: h.shape[0]], 8) == 7, crossing, h), 1)
            return he, hw

        def crossing_of(rows_of, slots):
            out = None
            for e in slots:
                moved = roll(rows_of(e), e * 8)
                if out is None:
                    out = moved
                else:
                    at = lane[: moved.shape[0]]
                    out = jnp.where((at == e * 8) | (at == e * 8 - 1), moved, out)
            return out

        def shifted(v, rim, e):
            near = lane[: v.shape[0]]
            side = roll(rim, -e * 8)
            ve = roll(jnp.where(near == 0, side, v), -1)
            vw = roll(jnp.where(near == width - 1, side, v), 1)
            return ve, vw

        slots_all = range(low, high + 1)

        def level_row(ref_value, at):
            return ref_value[at : at + 1, :]

        h_all = halo_a[...]
        h_ke, h_kn, h_w = (level_row(h_all, at) for at in (ke_at, kn_at, wet_at))
        f_ke = {e: field_a[e, ke_at : ke_at + 1, :] for e in slots_all}
        f_kn = {e: field_a[e, kn_at : kn_at + 1, :] for e in slots_all}
        f_w = {e: field_a[e, wet_at : wet_at + 1, :] for e in slots_all}
        hw_east, _ = shifted_rim(h_w, crossing_of(lambda e: f_w[e], slots_all))
        hke_east, _ = shifted_rim(h_ke, crossing_of(lambda e: f_ke[e], slots_all))
        beyond = (lane1 >= after * 8 - 4) & is_top
        fold_row = (lane1 >= top_slot * 8 - 4) & (lane1 < after * 8 - 4) & is_top
        h_e = jnp.where(beyond, hke_east, h_ke) * h_w * hw_east
        kn_up = roll(h_kn, -8)
        h_n = jnp.where(beyond, kn_up, jnp.where(fold_row, 0.5 * (h_kn + kn_up), h_kn)) * h_w * roll(h_w, -8)
        face_e, face_n = {}, {}
        for e in slots_all:
            w_east, _ = shifted(f_w[e], h_w, e)
            ke = f_ke[e]
            if e >= after:
                ke = jnp.where(is_top, shifted(ke, h_ke, e)[0], ke)
            face_e[e] = ke * f_w[e] * w_east
            if e < high:
                kn = f_kn[e]
                if e >= after:
                    kn = jnp.where(is_top, f_kn[e + 1], kn)
                elif e == top_slot:
                    kn = jnp.where(is_top, 0.5 * (kn + f_kn[e + 1]), kn)
                face_n[e] = kn * f_w[e] * f_w[e + 1]
        _, h_west = shifted_rim(h_e, crossing_of(lambda e: face_e[e], slots_all))
        h_s = roll(h_n, 8)
        for k, value in enumerate((1.0 - h_e - h_west - h_n - h_s, h_e, h_west, h_n, h_s)):
            hcoef[k : k + 1, :] = value
        for e in range(low + 1, high):
            _, f_west = shifted(face_e[e], h_e, e)
            center = 1.0 - face_e[e] - f_west - face_n[e] - face_n[e - 1]
            for k, value in enumerate((center, face_e[e], f_west, face_n[e], face_n[e - 1])):
                coef[e, k : k + 1, :] = value

        def diffuse(src, dst, hsrc, hdst, lo, hi, rim=True):
            h = hsrc[...]
            if rim:
                crossing = crossing_of(lambda e: src[e], range(lo, hi + 1))
                he, hw = shifted_rim(h, crossing)
                hdst[...] = (
                    hcoef[0:1, :] * h + hcoef[1:2, :] * he + hcoef[2:3, :] * hw
                    + hcoef[3:4, :] * roll(h, -8) + hcoef[4:5, :] * roll(h, 8)
                )
            for e in range(lo, hi + 1):
                v = src[e]
                ve, vw = shifted(v, h, e)
                dst[e] = (
                    coef[e, 0:1, :] * v + coef[e, 1:2, :] * ve + coef[e, 2:3, :] * vw
                    + coef[e, 3:4, :] * src[e + 1] + coef[e, 4:5, :] * src[e - 1]
                )

        to_west.wait_send()
        to_east.wait_send()

        @pl.when(jnp.logical_not(is_top))
        def _():
            to_north.wait_send()
            legs_a[0].wait_send()

        @pl.when(jnp.logical_not(is_bottom))
        def _():
            to_south.wait_send()
            legs_a[1].wait_send()

        @pl.when(is_top)
        def _():
            pltpu.make_async_remote_copy(
                src_ref=flip_a, dst_ref=north_a, send_sem=send_sem.at[2], recv_sem=recv_sem.at[3],
                device_id=mirror, device_id_type=MESH,
            ).wait_send()
            legs_a[2].wait_send()

        diffuse(field_a, field_b, halo_a, halo_b, first - 2, after + 2)
        diffuse(field_b, field_a, halo_b, halo_a, first - 1, after + 1)
        diffuse(field_a, field_b, halo_a, halo_b, first, after)

        rim_used = (sub8 == 0) & (lane >= first * 8) & (lane <= after * 8)
        profile = mm(jnp.where(rim_used, halo_b[...], 0.0), rim_weight)
        for j in range(rows + 1):
            profile = profile + row_weights[j] * mm(field_b[first + j], col_weight)
        weighted = rinv_pad[...] * mm(eof, profile)
        back = mm(eof_t, weighted)

        for j in range(rows + 1):
            spread[j] = mm(row_weights[j] * back, col_weight, ((1,), (1,)))
        over = mm(back, rim_weight, ((1,), (1,)))
        own = packed(spread, range(first, after + 1), first)
        over_slots = (sub8 == 3) & (lane >= first * 8) & (lane <= after * 8 + 3)
        pack_b[...] = jnp.where(over_slots, roll(over, 3), jnp.where(sub8 == 4, 0.0, own))
        to_west_b = remote(pack_b, east_b, 6, west)
        to_east_b = remote(pack_b, west_b, 7, east)
        to_west_b.start()
        to_east_b.start()
        to_north_b = remote(spread.at[pl.ds(rows - 3, 4)], south_b, 8, north)
        to_south_b = remote(spread.at[pl.ds(0, 3)], north_b, 9, south)
        to_mirror_b = pltpu.make_async_remote_copy(
            src_ref=flip_b, dst_ref=north_b, send_sem=send_sem.at[8], recv_sem=recv_sem.at[9],
            device_id=mirror, device_id_type=MESH,
        )

        @pl.when(jnp.logical_not(is_top))
        def _():
            to_north_b.start()

        @pl.when(jnp.logical_not(is_bottom))
        def _():
            to_south_b.start()

        @pl.when(is_top)
        def _():
            for k in range(3):
                flip_b[k] = flip(spread[rows - 1 - k])
            to_mirror_b.start()

        to_west_b.wait_recv()
        to_east_b.wait_recv()
        comb_b[...] = jnp.where(sub8 < 3, east_b[...], west_b[...]) + jnp.where(sub8 == 0, over, 0.0)
        legs_b = second_leg(comb_b, flipc_b, cnorth_b, csouth_b, 10)

        @pl.when(is_bottom)
        def _():
            south_b[...] = jnp.zeros_like(south_b)
            csouth_b[...] = jnp.zeros_like(csouth_b)

        to_south_b.wait_recv()
        legs_b[1].wait_recv()

        @pl.when(jnp.logical_not(is_bottom))
        def _():
            to_north_b.wait_recv()
            legs_b[0].wait_recv()

        in_north_b = (lane >= after * 8 - 4) & (lane < (after + 3) * 8 - 4)
        in_south_b = (lane >= (first - 3) * 8 - 4) & (lane < (first + 1) * 8 - 4)
        rim = (
            comb_b[...] + jnp.where(in_north_b, roll(cnorth_b[...], 64), 0.0)
            + jnp.where(in_south_b, roll(csouth_b[...], 64), 0.0)
        )
        halo_a[...] = rim
        for e in range(first - 3, after + 3):
            if e < first:
                v = south_b[e - first + 3]
            elif e == first:
                v = spread[0] + south_b[3]
            elif e < after:
                v = spread[e - first]
            elif e == after:
                v = spread[rows] + north_b[0]
            else:
                v = north_b[e - after]
            v = v + jnp.where(lane == 0, roll(rim, -e * 8 - 3), 0.0)
            if e >= after:
                v = v + jnp.where(lane == width - 1, roll(rim, -e * 8 + 3), 0.0)
            field_a[e] = v

        diffuse(field_a, field_b, halo_a, halo_b, first - 2, after + 1)
        diffuse(field_b, field_a, halo_b, halo_a, first - 1, after)
        diffuse(field_a, field_b, halo_a, halo_b, first, after - 1, rim=False)

        sums = [jnp.zeros((levels, width), F32) for _ in range(4)]
        for j in range(rows):
            d = d_ref[:, j, :]
            r = r_ref[:, j, :]
            im = d + field_b[first + j, 0:levels, :]
            image[j, 0:levels, :] = im
            for k, term in enumerate((r * r, d * im, r * im, im * im)):
                sums[k] = sums[k] + term
        for k in range(4):
            red[k : k + 1, :] = jnp.sum(sums[k], axis=0, keepdims=True)
        red[4:8, :] = jnp.zeros((4, width), F32)

        def lon_copy(k):
            return pltpu.make_async_remote_copy(
                src_ref=red, dst_ref=lon_in.at[k], send_sem=lon_send.at[k], recv_sem=lon_recv.at[k],
                device_id=(lax.rem(lon + k, n_lon), lat), device_id_type=MESH,
            )

        def lat_copy(k):
            return pltpu.make_async_remote_copy(
                src_ref=red2, dst_ref=lat_in.at[k], send_sem=lat_send.at[k], recv_sem=lat_recv.at[k],
                device_id=(lon, lax.rem(lat + k, n_lat)), device_id_type=MESH,
            )

        for k in range(1, n_lon):
            lon_copy(k).start()
        total = red[...]
        for k in range(1, n_lon):
            lon_copy(k).wait_recv()
        for k in range(1, n_lon):
            total = total + lon_in[k]
        red2[...] = total
        for k in range(1, n_lat):
            lat_copy(k).start()
        for k in range(1, n_lat):
            lat_copy(k).wait_recv()
        for k in range(1, n_lat):
            total = total + lat_in[k]
        scalars = jnp.sum(total, axis=1, keepdims=True)
        old_norm = scalars[0:1]
        curvature = scalars[1:2]
        cross = scalars[2:3]
        square = scalars[3:4]
        step = old_norm / curvature
        new_norm = old_norm - 2.0 * (step * cross) + step * (step * square)
        ratio = new_norm / old_norm
        step_ref[...] = step
        for j in range(rows):
            nr = r_ref[:, j, :] - step * image[j, 0:levels, :]
            nr_ref[:, j, :] = nr
            nd_ref[:, j, :] = nr + ratio * d_ref[:, j, :]

        to_west_b.wait_send()
        to_east_b.wait_send()

        @pl.when(jnp.logical_not(is_top))
        def _():
            to_north_b.wait_send()
            legs_b[0].wait_send()

        @pl.when(jnp.logical_not(is_bottom))
        def _():
            to_south_b.wait_send()
            legs_b[1].wait_send()

        @pl.when(is_top)
        def _():
            to_mirror_b.wait_send()
            legs_b[2].wait_send()

        for k in range(1, n_lon):
            lon_copy(k).wait_send()
        for k in range(1, n_lat):
            lat_copy(k).wait_send()

    def tile(*lead):
        return pltpu.VMEM((*lead, lp, width), F32)

    ext = rows + 8
    scratch = [
        tile(ext), tile(ext), tile(), tile(), pltpu.VMEM((ext, 8, width), F32), pltpu.VMEM((8, width), F32),
        tile(), tile(), tile(), tile(), tile(4), tile(), tile(4), tile(3), tile(), tile(),
        tile(rows + 1), tile(), tile(), tile(), tile(), tile(3), tile(), tile(3), tile(4), tile(), tile(),
        pltpu.VMEM((width, width), F32), pltpu.VMEM((lp, n_obs), F32), tile(rows),
        pltpu.VMEM((8, width), F32), pltpu.VMEM((n_lon, 8, width), F32),
        pltpu.VMEM((8, width), F32), pltpu.VMEM((n_lat, 8, width), F32),
        pltpu.SemaphoreType.DMA((12,)), pltpu.SemaphoreType.DMA((12,)),
        pltpu.SemaphoreType.DMA((n_lon,)), pltpu.SemaphoreType.DMA((n_lon,)),
        pltpu.SemaphoreType.DMA((n_lat,)), pltpu.SemaphoreType.DMA((n_lat,)),
    ]
    vmem = pl.BlockSpec(memory_space=pltpu.VMEM)
    return pl.pallas_call(
        kernel,
        out_shape=(
            jax.ShapeDtypeStruct((levels, rows, width), F32),
            jax.ShapeDtypeStruct((levels, rows, width), F32),
            jax.ShapeDtypeStruct((1, 1), F32),
        ),
        in_specs=[vmem] * 9,
        out_specs=(vmem, vmem, vmem),
        scratch_shapes=scratch,
        compiler_params=pltpu.CompilerParams(
            collective_id=0, has_side_effects=True, vmem_limit_bytes=48 * 1024 * 1024
        ),
    )


def solution(mesh):
    n_lon, n_lat = mesh.shape["lon"], mesh.shape["lat"]

    def per_device(direction, residual, eof_basis, kappa_east, kappa_north, wet_mask, obs_base, obs_frac, obs_rinv):
        levels, rows, width = direction.shape
        n_obs = obs_base.shape[-1]
        call = make_kernel(n_lon, n_lat, levels, rows, width, n_obs)
        new_residual, new_direction, step = call(
            direction, residual, eof_basis, kappa_east, kappa_north, wet_mask,
            obs_base.reshape(1, n_obs), obs_frac.reshape(2, n_obs), obs_rinv.reshape(levels, n_obs),
        )
        return new_residual, new_direction, step.reshape(())

    return jax.shard_map(
        per_device,
        mesh=mesh,
        in_specs=(
            P(None, "lat", "lon"),
            P(None, "lat", "lon"),
            P(),
            P("lat", "lon"),
            P("lat", "lon"),
            P("lat", "lon"),
            P("lat", "lon", None),
            P(None, "lat", "lon", None),
            P(None, "lat", "lon", None),
        ),
        out_specs=(P(None, "lat", "lon"), P(None, "lat", "lon"), P()),
        check_vma=False,
    )
```

time: 282 us -> 44.2 us (0.16)
  waiting for transfers between devices: 96 us -> 0 us
  blocking collectives: 80 us -> 0 us
  starting transfers between devices: 66.1 us -> 0 us
  Pallas kernels: 0 us -> 35.9 us
  other arithmetic: 18.9 us -> 0 us
  local copies, waits for them, and re-layouts: 14.2 us -> 5.65 us
  between operations: 5.25 us -> 2.37 us
    ppermute x55 -> x0, waiting for transfers between devices: 96 us -> none  [the longest x16 61.4 us: padded_2(): before = lax.ppermute(last, axis, up)]
    psum x2 -> x0, blocking collectives: 80 us -> none  [the longest x1 42.4 us: per_device(): new_norm = lax.psum(jnp.sum(new_residual * new_residual), ('lon', 'lat'))]
    ppermute x55 -> x0, starting transfers between devices: 66.1 us -> none  [the longest x16 48.6 us: padded_2(): after = lax.ppermute(leading, axis, down)]
    pallas_call x0 -> x1, Pallas kernels: none -> 35.9 us  [per_device(): call(direction, residual, eof_basis, kappa_east, kappa_north, wet_mask, o...]
    scatter-add x11 -> x0, other arithmetic: 8.73 us -> none  [the longest x4 8.57 us: per_device(): spread.at[:, corner_index[corner]]]
    scatter-add x1 -> x0, local copies, waits for them, and re-layouts: 3.56 us -> none  [per_device(): spread.at[:, 1:lat_cells + 2, 1].add(passed_along(east_part, 'lon', 1))]
    add x14 -> x0, other arithmetic: 3.23 us -> none  [the longest x6 2.08 us: diffuse(): change = change + south_face * (padded[:, :-2, 1:-1] - values)]
    gather x4 -> x0, local copies, waits for them, and re-layouts: 2.93 us -> none  [per_device(): jnp.take(flat_field, corner_index[corner], axis=1)]
  transfers between devices with their start and end apart: 55 -> 0, of which waited for: 31 -> 0; matrix products, arithmetic and copies ran while one was open for 3% -> 0% of each run, Pallas kernels for 0% -> 0%
where the time goes in v1:
time: 44.2 us; the launch traced here: 43.9 us
  Pallas kernels  35.9 us (81%)
  local copies, waits for them, and re-layouts  5.65 us (13%)
  between operations  2.37 us (5%)
    pallas_call x1, Pallas kernels, per_device(): call(direction, residual, eof_basis, kappa_east, kappa_north, wet_mask, o...  35.9 us
    unnamed x18, local copies, waits for them, and re-layouts  5.65 us

profile of v1, /device:TPU:0, one launch (start us, length us, event | category | flops | bytes accessed | tf_op | source)
XLA Modules:
  0.0 43.9 jit_solution(15997586158985586726)
XLA Ops:
  0.6 0.7 %copy.17 = f32[2,1,1,256]{3,0,1,2:T(2,128)S(1)} copy(f32[2,1,1,256]{3,2,1,0:T(1,128)} %param.16) | data formatting | bytes 4096
  1.3 0.0 copy-start.2
  1.3 0.0 copy-start.3
  1.3 0.0 copy-start.4
  1.3 0.0 copy-start.5
  1.3 0.9 %copy.16 = f32[75,1,1,256]{3,0,1,2:T(8,128)S(1)} copy(f32[75,1,1,256]{3,2,1,0:T(1,128)} %param.17) | data formatting | bytes 153600
  2.3 0.0 copy-start.6
  2.3 0.0 copy-done.2
  2.3 0.0 copy-done.3
  2.3 0.0 copy-done.4
  2.3 0.0 copy-done.5
  2.3 0.6 %copy-done.6 = s32[1,1,256]{2,1,0:T(1,128)S(1)} copy-done((s32[1,1,256]{2,1,0:T(1,128)S(1)}, s32[1,1,256]{2,1,0:T(1,128)}, u32[]{:S(2)}) %copy-start.6) | copy-done | bytes 1048
  3.0 0.0 copy-start
  3.0 1.0 %copy-done = f32[75,8,128]{2,1,0:T(8,128)S(1)} copy-done((f32[75,8,128]{2,1,0:T(8,128)S(1)}, f32[75,8,128]{2,1,0:T(8,128)}, u32[]{:S(2)}) %copy-start) | copy-done | bytes 307224
  3.9 0.0 copy-start.1
  3.9 1.0 %copy-done.1 = f32[75,8,128]{2,1,0:T(8,128)S(1)} copy-done((f32[75,8,128]{2,1,0:T(8,128)S(1)}, f32[75,8,128]{2,1,0:T(8,128)}, u32[]{:S(2)}) %copy-start.1) | copy-done | bytes 307224
  4.9 35.9 %shard_map.112 = (f32[75,8,128]{2,1,0:T(8,128)S(1)}, f32[75,8,128]{2,1,0:T(8,128)S(1)}, f32[1,1]{1,0:T(1,128)}) custom-call(f32[75,8,128]{2,1,0:T(8,128)S(1)} %copy-done, f32[75,8,128]{2,1,0:T(8,128)S(1)} %copy-done.1, f32[75,75]{1,0:T(8,128)S(1)} %copy-done.2, f32[8,128]{1,0:T(8,128)S(1)} %copy-done.3, f32[8,128]{1,0:T(8,128)S(1)} %copy-done.4, ...), custom_call_target="tpu_custom_call" | custom-call | tf_op jit(solution)/shard_map/pallas_call | solution.py:514
  40.8 0.7 %copy.21 = f32[75,8,128]{2,1,0:T(8,128)} copy(f32[75,8,128]{2,1,0:T(8,128)S(1)} %get-tuple-element.12) | data formatting | bytes 614400
  41.5 0.7 %copy.22 = f32[75,8,128]{2,1,0:T(8,128)} copy(f32[75,8,128]{2,1,0:T(8,128)S(1)} %get-tuple-element.13) | data formatting | bytes 614400
Async XLA Ops:
  1.3 1.0 %copy-start.2 = (f32[75,75]{1,0:T(8,128)S(1)}, f32[75,75]{1,0:T(8,128)}, u32[]{:S(2)}) copy-start(f32[75,75]{1,0:T(8,128)} %eof_ref.1) | copy-start | bytes 67504
  1.3 1.0 %copy-start.3 = (f32[8,128]{1,0:T(8,128)S(1)}, f32[8,128]{1,0:T(8,128)}, u32[]{:S(2)}) copy-start(f32[8,128]{1,0:T(8,128)} %ke_ref.1) | copy-start | bytes 12292
  1.3 1.0 %copy-start.4 = (f32[8,128]{1,0:T(8,128)S(1)}, f32[8,128]{1,0:T(8,128)}, u32[]{:S(2)}) copy-start(f32[8,128]{1,0:T(8,128)} %kn_ref.1) | copy-start | bytes 12292
  1.3 1.0 %copy-start.5 = (s32[8,128]{1,0:T(8,128)S(1)}, s32[8,128]{1,0:T(8,128)}, u32[]{:S(2)}) copy-start(s32[8,128]{1,0:T(8,128)} %wet_ref.1) | copy-start | bytes 12292
  2.3 0.7 %copy-start.6 = (s32[1,1,256]{2,1,0:T(1,128)S(1)}, s32[1,1,256]{2,1,0:T(1,128)}, u32[]{:S(2)}) copy-start(s32[1,1,256]{2,1,0:T(1,128)} %param.15) | copy-start | bytes 3076
  3.0 1.0 %copy-start = (f32[75,8,128]{2,1,0:T(8,128)S(1)}, f32[75,8,128]{2,1,0:T(8,128)}, u32[]{:S(2)}) copy-start(f32[75,8,128]{2,1,0:T(8,128)} %d_ref.1) | copy-start | bytes 921604
  3.9 1.0 %copy-start.1 = (f32[75,8,128]{2,1,0:T(8,128)S(1)}, f32[75,8,128]{2,1,0:T(8,128)}, u32[]{:S(2)}) copy-start(f32[75,8,128]{2,1,0:T(8,128)} %r_ref.1) | copy-start | bytes 921604

commit v2 on v1

--- a/solution.py
+++ b/solution.py
@@ -9,10 +9,23 @@
 MESH = pl.DeviceIdType.MESH
 
 
+BF16 = jnp.bfloat16
+
+
+def parts(x, count=2):
+    out = []
+    for _ in range(count):
+        part = x.astype(BF16)
+        out.append(part)
+        x = x - part.astype(F32)
+    return out
+
+
 def mm(a, b, dims=((1,), (0,))):
-    return lax.dot_general(
-        a, b, (dims, ((), ())), precision=lax.Precision.HIGHEST, preferred_element_type=F32
-    )
+    def one(x, y):
+        return lax.dot_general(x, y, (dims, ((), ())), preferred_element_type=F32)
+
+    return one(a[0], b[0]) + (one(a[0], b[1]) + one(a[1], b[0]))
 
 
 def make_kernel(n_lon, n_lat, levels, rows, width, n_obs):
@@ -27,14 +40,28 @@
         shift = shift % width
         return x if shift == 0 else pltpu.roll(x, shift, 1)
 
+    pieces = n_obs // width
+    pair = n_lon // 2
+    n_peers = pair * n_lat
+    everyone = [(2 * a, b) for a in range(pair) for b in range(n_lat) if a or b]
+    if n_peers <= 32:
+        phases = [everyone]
+    else:
+        phases = [[p for p in everyone if p[1] == 0], [p for p in everyone if p[0] == 0]]
+    greeted = [(a, 0) for a in range(1, n_lon)] + [(0, b) for b in range(1, n_lat)]
+    if len(phases) == 1:
+        greeted += [p for p in everyone if p[0] and p[1]]
+    n_copies = 1 + sum(len(p) for p in phases)
+
     def kernel(
-        d_ref, r_ref, eof_ref, ke_ref, kn_ref, wet_ref, base_ref, frac_ref, rinv_ref,
+        d_hbm, r_hbm, eof_hbm, ke_hbm, kn_hbm, wet_hbm, base_hbm, frac_hbm, rinv_hbm,
         nr_ref, nd_ref, step_ref,
         field_a, field_b, halo_a, halo_b, coef, hcoef,
         pack_a, east_a, west_a, comb_a, flip_a, flipc_a, north_a, south_a, cnorth_a, csouth_a,
         spread, pack_b, east_b, west_b, comb_b, flip_b, flipc_b, north_b, south_b, cnorth_b, csouth_b,
-        eof_pad, rinv_pad, image, red, lon_in, red2, lat_in,
-        send_sem, recv_sem, lon_send, lon_recv, lat_send, lat_recv,
+        eof_pad, rinv_pad, image, red, pair_in, sums_in, sums_in2,
+        d_ref, r_ref, eof_ref, ke_ref, kn_ref, wet_ref, base_ref, frac_ref, rinv_ref,
+        send_sem, recv_sem, red_send, red_recv, load_sem,
     ):
         lon = lax.axis_index("lon")
         lat = lax.axis_index("lat")
@@ -50,10 +77,21 @@
         sub8 = lax.rem(lane, 8)
 
         barrier = pltpu.get_barrier_semaphore()
-        for k in range(1, n_lon):
-            pl.semaphore_signal(barrier, inc=1, device_id=(lax.rem(lon + k, n_lon), lat), device_id_type=MESH)
-        for k in range(1, n_lat):
-            pl.semaphore_signal(barrier, inc=1, device_id=(lon, lax.rem(lat + k, n_lat)), device_id_type=MESH)
+        for a, b in greeted:
+            pl.semaphore_signal(
+                barrier, inc=1, device_id=(lax.rem(lon + a, n_lon), lax.rem(lat + b, n_lat)), device_id_type=MESH
+            )
+        loads = [
+            pltpu.make_async_copy(src, dst, load_sem.at[k])
+            for k, (src, dst) in enumerate((
+                (d_hbm, d_ref), (ke_hbm, ke_ref), (kn_hbm, kn_ref), (wet_hbm, wet_ref), (eof_hbm, eof_ref),
+                (base_hbm, base_ref), (frac_hbm, frac_ref), (rinv_hbm, rinv_ref), (r_hbm, r_ref),
+            ))
+        ]
+        for load in loads:
+            load.start()
+        for load in loads[:4]:
+            load.wait()
 
         for j in range(rows):
             e = first + j
@@ -76,13 +114,13 @@
 
         row_id = lax.broadcasted_iota(jnp.int32, (width, width), 0)
         col_id = lax.broadcasted_iota(jnp.int32, (width, width), 1)
-        reverse = (row_id + col_id == width - 1).astype(F32)
+        reverse = (row_id + col_id == width - 1).astype(F32).astype(BF16)
 
         def flip(x):
-            return mm(x, reverse)
+            return sum(jnp.dot(part, reverse, preferred_element_type=F32) for part in parts(x, 3)[::-1])
 
         def flip_packed(x):
-            return roll(mm(x, reverse), (2 * top_slot + 1) * 8 - 64 - width)
+            return roll(flip(x), (2 * top_slot + 1) * 8 - 64 - width)
 
         def remote(src, dst, index, device):
             return pltpu.make_async_remote_copy(
@@ -91,7 +129,7 @@
             )
 
         pack_a[...] = packed(field_a, range(first, after))
-        pl.semaphore_wait(barrier, n_lon + n_lat - 2)
+        pl.semaphore_wait(barrier, len(greeted))
 
         to_west = remote(pack_a, east_a, 0, west)
         to_east = remote(pack_a, west_a, 1, east)
@@ -117,9 +155,11 @@
                 device_id=mirror, device_id_type=MESH,
             ).start()
 
-        base = base_ref[...]
-        lat_frac = frac_ref[0:1, :]
-        lon_frac = frac_ref[1:2, :]
+        for load in loads[4:8]:
+            load.wait()
+        base = jnp.concatenate([base_ref[k : k + 1, :] for k in range(pieces)], axis=1)
+        lat_frac = jnp.concatenate([frac_ref[k : k + 1, :] for k in range(pieces)], axis=1)
+        lon_frac = jnp.concatenate([frac_ref[pieces + k : pieces + k + 1, :] for k in range(pieces)], axis=1)
         base_row = jnp.zeros_like(base)
         for j in range(1, rows):
             base_row = base_row + (base >= j * width).astype(jnp.int32)
@@ -144,10 +184,13 @@
         eof_pad[...] = jnp.zeros_like(eof_pad)
         eof_pad[0:levels, 0:levels] = eof_ref[...]
         rinv_pad[levels - levels % 8 : lp, :] = jnp.zeros((lp - (levels - levels % 8), n_obs), F32)
-        rinv_pad[0:levels, :] = rinv_ref[...]
+        for k in range(pieces):
+            rinv_pad[0:levels, k * width : (k + 1) * width] = rinv_ref[:, k, :]
         eof_full = eof_pad[...]
-        eof = eof_full[:lp, :lp]
-        eof_t = eof_full.T[:lp, :lp]
+        eof = parts(eof_full[:lp, :lp])
+        eof_t = parts(eof_full.T[:lp, :lp])
+        col_parts = parts(col_weight)
+        rim_parts = parts(rim_weight)
 
         def second_leg(comb, flipc, cnorth, csouth, start):
             legs = (
@@ -315,15 +358,16 @@
         diffuse(field_a, field_b, halo_a, halo_b, first, after)
 
         rim_used = (sub8 == 0) & (lane >= first * 8) & (lane <= after * 8)
-        profile = mm(jnp.where(rim_used, halo_b[...], 0.0), rim_weight)
+        profile = mm(parts(jnp.where(rim_used, halo_b[...], 0.0)), rim_parts)
+        along = mm(parts(field_b[first : after + 1].reshape((rows + 1) * lp, width)), col_parts)
         for j in range(rows + 1):
-            profile = profile + row_weights[j] * mm(field_b[first + j], col_weight)
-        weighted = rinv_pad[...] * mm(eof, profile)
-        back = mm(eof_t, weighted)
-
-        for j in range(rows + 1):
-            spread[j] = mm(row_weights[j] * back, col_weight, ((1,), (1,)))
-        over = mm(back, rim_weight, ((1,), (1,)))
+            profile = profile + row_weights[j] * along[j * lp : (j + 1) * lp]
+        weighted = rinv_pad[...] * mm(eof, parts(profile))
+        back = mm(eof_t, parts(weighted))
+
+        by_row = jnp.concatenate([row_weights[j] * back for j in range(rows + 1)], axis=0)
+        spread[...] = mm(parts(by_row), col_parts, ((1,), (1,))).reshape(rows + 1, lp, width)
+        over = mm(parts(back), rim_parts, ((1,), (1,)))
         own = packed(spread, range(first, after + 1), first)
         over_slots = (sub8 == 3) & (lane >= first * 8) & (lane <= after * 8 + 3)
         pack_b[...] = jnp.where(over_slots, roll(over, 3), jnp.where(sub8 == 4, 0.0, own))
@@ -397,6 +441,7 @@
         diffuse(field_b, field_a, halo_b, halo_a, first - 1, after)
         diffuse(field_a, field_b, halo_a, halo_b, first, after - 1, rim=False)
 
+        loads[8].wait()
         sums = [jnp.zeros((levels, width), F32) for _ in range(4)]
         for j in range(rows):
             d = d_ref[:, j, :]
@@ -409,32 +454,38 @@
             red[k : k + 1, :] = jnp.sum(sums[k], axis=0, keepdims=True)
         red[4:8, :] = jnp.zeros((4, width), F32)
 
-        def lon_copy(k):
-            return pltpu.make_async_remote_copy(
-                src_ref=red, dst_ref=lon_in.at[k], send_sem=lon_send.at[k], recv_sem=lon_recv.at[k],
-                device_id=(lax.rem(lon + k, n_lon), lat), device_id_type=MESH,
-            )
-
-        def lat_copy(k):
-            return pltpu.make_async_remote_copy(
-                src_ref=red2, dst_ref=lat_in.at[k], send_sem=lat_send.at[k], recv_sem=lat_recv.at[k],
-                device_id=(lon, lax.rem(lat + k, n_lat)), device_id_type=MESH,
-            )
-
-        for k in range(1, n_lon):
-            lon_copy(k).start()
-        total = red[...]
-        for k in range(1, n_lon):
-            lon_copy(k).wait_recv()
-        for k in range(1, n_lon):
-            total = total + lon_in[k]
-        red2[...] = total
-        for k in range(1, n_lat):
-            lat_copy(k).start()
-        for k in range(1, n_lat):
-            lat_copy(k).wait_recv()
-        for k in range(1, n_lat):
-            total = total + lat_in[k]
+        with_pair = pltpu.make_async_remote_copy(
+            src_ref=red, dst_ref=pair_in, send_sem=red_send.at[0], recv_sem=red_recv.at[0],
+            device_id=(lon + 1 - 2 * lax.rem(lon, 2), lat), device_id_type=MESH,
+        )
+        with_pair.start()
+        sent = [with_pair]
+        with_pair.wait_recv()
+        total = red[...] + pair_in[...]
+        index = 1
+        for number, peers in enumerate(phases):
+            into = (sums_in, sums_in2)[number]
+            if len(phases) == 1:
+                slots, slot = n_peers, lax.div(lon, 2) * n_lat + lat
+            else:
+                slots, slot = (pair, lax.div(lon, 2)) if number == 0 else (n_lat, lat)
+            into[slot] = total
+            copies = []
+            for a, b in peers:
+                copies.append(pltpu.make_async_remote_copy(
+                    src_ref=into.at[slot], dst_ref=into.at[slot],
+                    send_sem=red_send.at[index], recv_sem=red_recv.at[index],
+                    device_id=(lax.rem(lon + a, n_lon), lax.rem(lat + b, n_lat)), device_id_type=MESH,
+                ))
+                index += 1
+            for copy in copies:
+                copy.start()
+            for copy in copies:
+                copy.wait_recv()
+            sent += copies
+            total = into[0]
+            for k in range(1, slots):
+                total = total + into[k]
         scalars = jnp.sum(total, axis=1, keepdims=True)
         old_norm = scalars[0:1]
         curvature = scalars[1:2]
@@ -467,10 +518,8 @@
             to_mirror_b.wait_send()
             legs_b[2].wait_send()
 
-        for k in range(1, n_lon):
-            lon_copy(k).wait_send()
-        for k in range(1, n_lat):
-            lat_copy(k).wait_send()
+        for copy in sent:
+            copy.wait_send()
 
     def tile(*lead):
         return pltpu.VMEM((*lead, lp, width), F32)
@@ -481,11 +530,15 @@
         tile(), tile(), tile(), tile(), tile(4), tile(), tile(4), tile(3), tile(), tile(),
         tile(rows + 1), tile(), tile(), tile(), tile(), tile(3), tile(), tile(3), tile(4), tile(), tile(),
         pltpu.VMEM((width, width), F32), pltpu.VMEM((lp, n_obs), F32), tile(rows),
-        pltpu.VMEM((8, width), F32), pltpu.VMEM((n_lon, 8, width), F32),
-        pltpu.VMEM((8, width), F32), pltpu.VMEM((n_lat, 8, width), F32),
+        pltpu.VMEM((8, width), F32), pltpu.VMEM((8, width), F32),
+        pltpu.VMEM((n_peers if len(phases) == 1 else pair, 8, width), F32), pltpu.VMEM((n_lat, 8, width), F32),
+        pltpu.VMEM((levels, rows, width), F32), pltpu.VMEM((levels, rows, width), F32),
+        pltpu.VMEM((levels, levels), F32), pltpu.VMEM((rows, width), F32), pltpu.VMEM((rows, width), F32),
+        pltpu.VMEM((rows, width), jnp.int32), pltpu.VMEM((pieces, width), jnp.int32),
+        pltpu.VMEM((2 * pieces, width), F32), pltpu.VMEM((levels, pieces, width), F32),
         pltpu.SemaphoreType.DMA((12,)), pltpu.SemaphoreType.DMA((12,)),
-        pltpu.SemaphoreType.DMA((n_lon,)), pltpu.SemaphoreType.DMA((n_lon,)),
-        pltpu.SemaphoreType.DMA((n_lat,)), pltpu.SemaphoreType.DMA((n_lat,)),
+        pltpu.SemaphoreType.DMA((n_copies,)), pltpu.SemaphoreType.DMA((n_copies,)),
+        pltpu.SemaphoreType.DMA((9,)),
     ]
     vmem = pl.BlockSpec(memory_space=pltpu.VMEM)
     return pl.pallas_call(
@@ -495,11 +548,11 @@
             jax.ShapeDtypeStruct((levels, rows, width), F32),
             jax.ShapeDtypeStruct((1, 1), F32),
         ),
-        in_specs=[vmem] * 9,
+        in_specs=[pl.BlockSpec(memory_space=pltpu.HBM)] * 9,
         out_specs=(vmem, vmem, vmem),
         scratch_shapes=scratch,
         compiler_params=pltpu.CompilerParams(
-            collective_id=0, has_side_effects=True, vmem_limit_bytes=48 * 1024 * 1024
+            collective_id=0, has_side_effects=True, vmem_limit_bytes=64 * 1024 * 1024 - 128 * 1024
         ),
     )
 
@@ -513,7 +566,8 @@
         call = make_kernel(n_lon, n_lat, levels, rows, width, n_obs)
         new_residual, new_direction, step = call(
             direction, residual, eof_basis, kappa_east, kappa_north, wet_mask,
-            obs_base.reshape(1, n_obs), obs_frac.reshape(2, n_obs), obs_rinv.reshape(levels, n_obs),
+            obs_base.reshape(n_obs // width, width), obs_frac.reshape(2 * n_obs // width, width),
+            obs_rinv.reshape(levels, n_obs // width, width),
         )
         return new_residual, new_direction, step.reshape(())
 

time: 44.2 us -> 39.9 us (0.903)
  local copies, waits for them, and re-layouts: 5.65 us -> 2.47 us
  Pallas kernels: 35.9 us -> 34.9 us
    unnamed x18 -> x4, local copies, waits for them, and re-layouts: 5.65 us -> 2.47 us
    pallas_call x1, Pallas kernels: 35.9 us -> 34.9 us  [per_device(): call(direction, residual, eof_basis, kappa_east, kappa_north, wet_mask, o...]
where the time goes in v2:
time: 39.9 us; the launch traced here: 39.8 us
  Pallas kernels  34.9 us (87%)
  local copies, waits for them, and re-layouts  2.47 us (6%)
  between operations  2.4 us (6%)
    pallas_call x1, Pallas kernels, per_device(): call(direction, residual, eof_basis, kappa_east, kappa_north, wet_mask, o...  34.9 us
    unnamed x4, local copies, waits for them, and re-layouts  2.47 us

profile of v2, /device:TPU:0, one launch (start us, length us, event | category | flops | bytes accessed | tf_op | source)
XLA Modules:
  0.0 39.8 jit_solution(16135520218070871623)
XLA Ops:
  0.6 34.9 %shard_map.112 = (f32[75,8,128]{2,1,0:T(8,128)}, f32[75,8,128]{2,1,0:T(8,128)}, f32[1,1]{1,0:T(1,128)}) custom-call(f32[75,8,128]{2,1,0:T(8,128)} %d_hbm.1, f32[75,8,128]{2,1,0:T(8,128)} %r_hbm.1, f32[75,75]{1,0:T(8,128)} %eof_hbm.1, f32[8,128]{1,0:T(8,128)} %ke_hbm.1, f32[8,128]{1,0:T(8,128)} %kn_hbm.1, s32[8,128]{1,0:T(8,128)} %wet_hbm.1, ...), custom_call_target="tpu_custom_call" | custom-call | tf_op jit(solution)/shard_map/pallas_call | solution.py:567
  35.5 0.0 copy-start
  35.5 1.7 %copy.15 = f32[75,8,128]{2,1,0:T(8,128)} copy(f32[75,8,128]{2,1,0:T(8,128)} %get-tuple-element.12) | data formatting | bytes 614400
  37.3 0.0 copy-done
  37.3 0.7 %copy.16 = f32[75,8,128]{2,1,0:T(8,128)} copy(f32[75,8,128]{2,1,0:T(8,128)S(1)} %copy-done) | data formatting | bytes 614400
Async XLA Ops:
  35.5 1.8 %copy-start = (f32[75,8,128]{2,1,0:T(8,128)S(1)}, f32[75,8,128]{2,1,0:T(8,128)}, u32[]{:S(2)}) copy-start(f32[75,8,128]{2,1,0:T(8,128)} %get-tuple-element.13) | copy-start | bytes 921604
